TPU v7x, 128 devices: a whole 4x4x4 slice. The times are simulated.
128 devices in a mesh: dp: 4 (over x), tensor: 32 (over y, z, core).
Axes of the slice: x: 4, y: 4, z: 4, core: 2. Of those that a mesh axis runs over, the one named last changes fastest.
Arguments:
- activations: bfloat16 [1024, 8192], P('dp', 'tensor'), may hold values from -6 to 6
- gate_weight: bfloat16 [8192, 28672], P('dp', 'tensor'), may hold values from -0.0625 to 0.0625
- up_weight: bfloat16 [8192, 28672], P('dp', 'tensor'), may hold values from -0.0625 to 0.0625
- group_mix: float32 [7, 7], replicated, may hold values from -2 to 2
- down_weight: bfloat16 [28672, 8192], P('tensor'), may hold values from -0.03125 to 0.03125
Outputs:
- ffn_out: bfloat16 [1024, 8192], P('dp', 'tensor')
All inputs are finite; a program needn't handle non-finite values.
Results may differ from a plain program's by a relative error of at most 0.0065.
Values may be sent and summed in bfloat16 or wider, within the bound.
A program may use at most 128 MiB of HBM per device.

v0:
```python
import math

import jax
import jax.numpy as jnp
from jax import lax
from jax.sharding import PartitionSpec as P


def swapped(array, axis, stride):
    return lax.ppermute(array, axis, [(i, i ^ 1 << stride) for i in range(lax.axis_size(axis))])


def sign_table(table_size):
    indices = jnp.arange(table_size, dtype=jnp.int32)
    common = indices[:, None] & indices[None, :]
    parity = jnp.zeros((table_size, table_size), jnp.int32)
    for bit_place in range(max(1, (table_size - 1).bit_length())):
        parity = parity ^ common >> bit_place & 1
    return (1 - 2 * parity).astype(jnp.float32)


def local_mix(rows_low, span_signs, group_mix, scale_factor):
    row_count = rows_low.shape[0]
    group_size = group_mix.shape[0]
    local_span = span_signs.shape[0]
    shaped = rows_low.reshape(row_count, local_span, group_size)
    signed = jnp.einsum("tbc,db->tdc", shaped, span_signs, preferred_element_type=jnp.float32)
    mixed = jnp.einsum("tdc,ac->tda", signed, group_mix, precision=lax.Precision.HIGHEST)
    return (mixed * scale_factor).reshape(row_count, local_span * group_size)


def local(activations, gate_weight, up_weight, group_mix, down_weight):
    shard_width = gate_weight.shape[1]
    tensor_count = lax.axis_size("tensor")
    group_size = group_mix.shape[0]
    local_span = shard_width // group_size
    scale_factor = 1.0 / math.sqrt(local_span * tensor_count)
    feature_rows = lax.all_gather(activations, "tensor", axis=1, tiled=True)
    quarter_rows = lax.all_to_all(feature_rows, "dp", split_axis=1, concat_axis=0, tiled=True)
    gate_part = jnp.dot(quarter_rows, gate_weight, preferred_element_type=jnp.float32)
    up_part = jnp.dot(quarter_rows, up_weight, preferred_element_type=jnp.float32)
    summed = lax.psum_scatter(
        jnp.concatenate([gate_part, up_part], axis=1), "dp", scatter_dimension=0, tiled=True
    )
    gate_sum = summed[:, :shard_width]
    up_sum = summed[:, shard_width:]
    hidden = (jax.nn.silu(gate_sum) * up_sum).astype(jnp.bfloat16)
    span_signs = sign_table(local_span).astype(jnp.bfloat16)
    mixed_rows = local_mix(hidden, span_signs, group_mix, scale_factor)
    own_index = lax.axis_index("tensor")
    for bit_place in range(tensor_count.bit_length() - 1):
        partner = swapped(mixed_rows, "tensor", bit_place)
        upper_half = own_index >> bit_place & 1 == 1
        mixed_rows = jnp.where(upper_half, partner - mixed_rows, mixed_rows + partner)
    rotated = mixed_rows.astype(jnp.bfloat16)
    down_terms = jnp.dot(rotated, down_weight, preferred_element_type=jnp.float32)
    return lax.psum_scatter(down_terms, "tensor", scatter_dimension=1, tiled=True).astype(
        jnp.bfloat16
    )


def solution(mesh):
    return jax.shard_map(
        local,
        mesh=mesh,
        in_specs=(P("dp", "tensor"), P("dp", "tensor"), P("dp", "tensor"), P(), P("tensor", None)),
        out_specs=P("dp", "tensor"),
        check_vma=False,
    )
```

profile of v0, /device:TPU:1, one launch (start us, length us, event | category | flops | bytes accessed | tf_op | source)
XLA Modules:
  0.0 412.5 jit_solution(11773133055998553026)
XLA Ops:
  6.5 1.7 copy.7
  8.3 51.4 %all-gather.2.cloned.1.call-done = bf16[256,8192]{0,1:T(8,128)(2,1)} async-done(((bf16[256,256]{0,1:T(8,128)(2,1)}), bf16[256,8192]{0,1:T(8,128)(2,1)}) %all-gather.2.cloned.1.call-update) | async-done | bytes 4194320 | tf_op jit(solution)/shard_map/all_gather | solution.py:38
  59.7 54.3 %all_to_all.19 = bf16[256,4,2048]{0,2,1:T(8,128)(2,1)} all-to-all(bf16[256,4,2048]{0,2,1:T(8,128)(2,1)} %bitcast.22), channel_id=1, replica_groups=mesh['dp'=4,'tensor'=32] {'dp'}, dimensions={1} | all-to-all | bytes 8388608 | tf_op jit(solution)/shard_map/all_to_all | solution.py:39
  114.0 6.3 %copy.8 = bf16[4,256,2048]{2,1,0:T(8,128)(2,1)} copy(bf16[4,256,2048]{1,2,0:T(8,128)(2,1)} %bitcast.21) | data formatting | bytes 8388608 | tf_op jit(solution)/shard_map/all_to_all | solution.py:39
  120.3 7.1 %fusion.22 = f32[1024,896]{0,1:T(8,128)S(1)} fusion(bf16[1024,2048]{1,0:T(8,128)(2,1)} %bitcast.23, bf16[2048,896]{1,0:T(8,128)(2,1)} %param.7), kind=kOutput, calls=%fused_computation.31 | convolution fusion | flops 3758096384 | bytes 11534336 | tf_op jit(solution)/shard_map/dot_general | solution.py:41
  127.4 4.3 %fusion.21 = f32[1024,896]{0,1:T(8,128)S(1)} fusion(bf16[1024,2048]{1,0:T(8,128)(2,1)S(1)} %bitcast.24, bf16[2048,896]{1,0:T(8,128)(2,1)S(1)} %copy-done.2), kind=kOutput, calls=%fused_computation.30 | convolution fusion | flops 3758096384 | bytes 11534336 | tf_op jit(solution)/shard_map/dot_general | solution.py:40
  131.7 3.7 pad_maximum_fusion
  135.4 70.6 %reduce-scatter.3.cloned.1.call-done = f32[256,1792]{0,1:T(8,128)} async-done(((f32[1024,1792]{0,1:T(8,128)}), f32[256,1792]{0,1:T(8,128)}) %reduce-scatter.3.cloned.1.call-update) | async-done | bytes 1835024 | tf_op jit(solution)/shard_map/reduce_scatter | solution.py:42
  206.0 1.7 fusion
  208.6 1.0 convolution_multiply_fusion
  209.6 0.6 copy.11
  210.3 0.7 collective-permute-start
  211.0 2.1 collective-permute-done
  213.3 1.3 collective-permute-start.1
  214.6 20.3 %collective-permute-done.1 = f32[256,896]{0,1:T(8,128)S(1)} collective-permute-done((f32[256,896]{0,1:T(8,128)S(1)}, f32[256,896]{0,1:T(8,128)S(1)}, u32[]{:S(2)}, u32[]{:S(2)}) %collective-permute-start.1) | collective-permute-done | bytes 917536 | tf_op jit(solution)/shard_map/ppermute | solution.py:10
  235.0 2.9 collective-permute-start.2
  238.0 19.3 %collective-permute-done.2 = f32[256,896]{0,1:T(8,128)S(1)} collective-permute-done((f32[256,896]{0,1:T(8,128)S(1)}, f32[256,896]{0,1:T(8,128)S(1)}, u32[]{:S(2)}, u32[]{:S(2)}) %collective-permute-start.2) | collective-permute-done | bytes 917536 | tf_op jit(solution)/shard_map/ppermute | solution.py:10
  257.4 1.4 collective-permute-start.3
  258.8 18.5 %collective-permute-done.3 = f32[256,896]{0,1:T(8,128)S(1)} collective-permute-done((f32[256,896]{0,1:T(8,128)S(1)}, f32[256,896]{0,1:T(8,128)S(1)}, u32[]{:S(2)}, u32[]{:S(2)}) %collective-permute-start.3) | collective-permute-done | bytes 917536 | tf_op jit(solution)/shard_map/ppermute | solution.py:10
  277.5 2.8 collective-permute-start.4
  280.3 18.4 %collective-permute-done.4 = f32[256,896]{0,1:T(8,128)S(1)} collective-permute-done((f32[256,896]{0,1:T(8,128)S(1)}, f32[256,896]{0,1:T(8,128)S(1)}, u32[]{:S(2)}, u32[]{:S(2)}) %collective-permute-start.4) | collective-permute-done | bytes 917536 | tf_op jit(solution)/shard_map/ppermute | solution.py:10
  298.6 12.1 %fusion.1 = f32[256,8192]{1,0:T(8,128)} fusion(bf16[896,8192]{1,0:T(8,128)(2,1)} %param.9, f32[256,896]{0,1:T(8,128)S(1)} %add_select_fusion, f32[256,896]{0,1:T(8,128)S(1)} %collective-permute-done.4, pred[]{:T(512)S(6)} %eq.15), kind=kOutput, calls=%fused_computation.10 | convolution fusion | flops 3759013888 | bytes 24903680 | tf_op jit(solution)/shard_map/dot_general | solution.py:56
  310.8 93.6 %reduce-scatter.5.cloned.1.call-done = f32[256,256]{1,0:T(8,128)} async-done(((f32[256,8192]{1,0:T(8,128)}), f32[256,256]{1,0:T(8,128)}) %reduce-scatter.5.cloned.1.call-update) | async-done | bytes 262160 | tf_op jit(solution)/shard_map/reduce_scatter | solution.py:57
  404.4 1.6 convert_element_type.19
  (20 shorter events, 1.6 us)
Async XLA Ops:
  6.5 202.1 %copy-start = (f32[7,7]{1,0:T(8,128)S(1)}, f32[7,7]{1,0:T(8,128)}, u32[]{:S(2)}) copy-start(f32[7,7]{1,0:T(8,128)} %param.8) | copy-start | bytes 592
  6.5 53.2 %all-gather.2.cloned.1.call-start = ((), (), s32[]{:S(2)}) async-start(), calls=%async_computation.3 | async-start | bytes 4325376 | tf_op jit(solution)/shard_map/all_gather | solution.py:38
  8.2 197.7 %reduce-scatter.3.cloned.1.call-start = ((), (), s32[]{:S(2)}) async-start(), calls=%async_computation.4 | async-start | bytes 9175040 | tf_op jit(solution)/shard_map/reduce_scatter | solution.py:42
  120.3 7.1 %copy-start.1 = (bf16[4,256,2048]{2,1,0:T(8,128)(2,1)S(1)}, bf16[4,256,2048]{2,1,0:T(8,128)(2,1)}, u32[]{:S(2)}) copy-start(bf16[4,256,2048]{2,1,0:T(8,128)(2,1)} %copy.8) | copy-start | bytes 12582916
  120.3 7.1 %copy-start.2 = (bf16[2048,896]{1,0:T(8,128)(2,1)S(1)}, bf16[2048,896]{1,0:T(8,128)(2,1)}, u32[]{:S(2)}) copy-start(bf16[2048,896]{1,0:T(8,128)(2,1)} %param.6) | copy-start | bytes 11010052
  135.4 269.0 %reduce-scatter.5.cloned.1.call-start = ((), (), s32[]{:S(2)}) async-start(), calls=%async_computation.5 | async-start | bytes 8650752 | tf_op jit(solution)/shard_map/reduce_scatter | solution.py:57
  210.3 2.8 collective-permute-start
  213.3 21.6 %collective-permute-start.1 = (f32[256,896]{0,1:T(8,128)S(1)}, f32[256,896]{0,1:T(8,128)S(1)}, u32[]{:S(2)}, u32[]{:S(2)}) collective-permute-start(f32[256,896]{0,1:T(8,128)S(1)} %add_select_fusion.3), channel_id=1, source_target_pairs={{0,2},{1,3},{2,0},{3,1},{4,6},{5,7},{6,4},{7,5},{8,10},{9,11},{10,... | collective-permute-start | bytes 2752520 | tf_op jit(solution)/shard_map/ppermute | solution.py:10
  235.0 22.2 %collective-permute-start.2 = (f32[256,896]{0,1:T(8,128)S(1)}, f32[256,896]{0,1:T(8,128)S(1)}, u32[]{:S(2)}, u32[]{:S(2)}) collective-permute-start(f32[256,896]{0,1:T(8,128)S(1)} %add_select_fusion.2), channel_id=1, source_target_pairs={{0,4},{1,5},{2,6},{3,7},{4,0},{5,1},{6,2},{7,3},{8,12},{9,13},{10,... | collective-permute-start | bytes 2752520 | tf_op jit(solution)/shard_map/ppermute | solution.py:10
  257.4 20.0 %collective-permute-start.3 = (f32[256,896]{0,1:T(8,128)S(1)}, f32[256,896]{0,1:T(8,128)S(1)}, u32[]{:S(2)}, u32[]{:S(2)}) collective-permute-start(f32[256,896]{0,1:T(8,128)S(1)} %add_select_fusion.1), channel_id=1, source_target_pairs={{0,8},{1,9},{2,10},{3,11},{4,12},{5,13},{6,14},{7,15},{8,0},{9,1},... | collective-permute-start | bytes 2752520 | tf_op jit(solution)/shard_map/ppermute | solution.py:10
  277.5 21.2 %collective-permute-start.4 = (f32[256,896]{0,1:T(8,128)S(1)}, f32[256,896]{0,1:T(8,128)S(1)}, u32[]{:S(2)}, u32[]{:S(2)}) collective-permute-start(f32[256,896]{0,1:T(8,128)S(1)} %add_select_fusion), channel_id=1, source_target_pairs={{0,16},{1,17},{2,18},{3,19},{4,20},{5,21},{6,22},{7,23},{8,24},{9,... | collective-permute-start | bytes 2752520 | tf_op jit(solution)/shard_map/ppermute | solution.py:10
Sparse Core Ops, SparseCore 0:
  9.6 50.0 all-gather.1
  135.5 70.4 reduce-scatter.2
  310.9 93.4 reduce-scatter.4
where the time goes:
time: 414 us; the launch traced here: 413 us
  waiting for transfers between devices  294 us (71%)
  blocking collectives  54.3 us (13%)
  matrix products  24.7 us (6%)
  between operations  13.2 us (3%)
  starting transfers between devices  9.32 us (2%)
  local copies, waits for them, and re-layouts  9.28 us (2%)
  other arithmetic  7.46 us (2%)
    reduce_scatter x1, waiting for transfers between devices, local(): lax.psum_scatter(down_terms, 'tensor', scatter_dimension=1, tiled=True)  93.6 us
    ppermute x5, waiting for transfers between devices, swapped(): lax.ppermute(array, axis, [(i, i ^ 1 << stride) for i in range(lax.axis_s...  78.6 us
    reduce_scatter x1, waiting for transfers between devices, local(): lax.psum_scatter(jnp.concatenate([gate_part, up_part], axis=1), 'dp', sca...  70.6 us
    all_to_all x1, blocking collectives, local(): lax.all_to_all(feature_rows, 'dp', split_axis=1, concat_axis=0, tiled=True)  54.3 us
    all_gather x1, waiting for transfers between devices, local(): feature_rows = lax.all_gather(activations, 'tensor', axis=1, tiled=True)  51.4 us
    dot_general x1, matrix products, local(): jnp.dot(rotated, down_weight, preferred_element_type=jnp.float32)  12.1 us
    ppermute x5, starting transfers between devices, swapped(): lax.ppermute(array, axis, [(i, i ^ 1 << stride) for i in range(lax.axis_s...  9.24 us
  transfers between devices with their start and end apart: 8, of which 8 were waited for; matrix products, arithmetic and copies ran while one was open for 0% of the time, Pallas kernels for 0%

commit v1 on v0

v1 whole, which is shorter than its diff:
```python
import jax
import jax.numpy as jnp
from jax import lax
from jax.experimental import pallas as pl
from jax.experimental.pallas import tpu as pltpu
from jax.sharding import PartitionSpec as P

MESH = pl.DeviceIdType.MESH
BF = jnp.bfloat16
F32 = jnp.float32

CHUNKS = 2
RB = 256 // CHUNKS
Q = RB // 4
HB = RB // 2
TILES = 7
SPAN = 896
GROUPS = 8


def wait_for(ref, sem):
    pltpu.make_async_copy(ref, ref, sem).wait()


def pack(pairs_of):
    out = []
    for i in range(0, GROUPS, 2):
        first = pairs_of[i]
        second = pairs_of[i + 1] if i + 1 < TILES else jnp.zeros_like(first)
        out.append(jnp.concatenate([first, second], axis=1).astype(BF))
    return jnp.concatenate(out, axis=1)


def unpack(packed):
    out = []
    for i in range(0, GROUPS, 2):
        pair = packed[:, i * 8 : i * 8 + 16, :].astype(F32)
        out.append(pair[:, :8, :].reshape(16 * 8, 128).astype(BF))
        if i + 1 < TILES:
            out.append(pair[:, 8:, :].reshape(16 * 8, 128).astype(BF))
    return jnp.concatenate(out, axis=1)


def kernel(
    act, gate, up, gm, down, out,
    wv, dv, af, pacc, own, nb, xo, xn, ro, rn,
    mhi, mlo, hs, hr, rs, rr, rot, ds, dk, dr, es, f1, g2, f2,
    w_sem, d_sem, a1_s, a1_r, ag_s, ag_r, xo_s, xo_r, xn_s, xn_r,
    h_s, h_r, ds_s, ds_r, e_s, e_r,
):
    x = lax.axis_index("dp")
    t = lax.axis_index("tensor")
    y, z, c = t // 8, (t // 2) % 4, t % 2
    p = t // 2
    sib = 1 - c
    xp, xm = (x + 1) % 4, (x + 3) % 4
    col = pl.multiple_of(c * 1024 + z * 256, 256)
    ccol = pl.multiple_of(c * 1024, 1024)

    def at(x_, y_, z_, c_):
        return (x_, y_ * 8 + z_ * 2 + c_)

    def send(src, dst, ss, rs_, dev):
        pltpu.make_async_remote_copy(
            src_ref=src, dst_ref=dst, send_sem=ss, recv_sem=rs_, device_id=dev, device_id_type=MESH
        ).start()

    for j in range(TILES):
        for cc in range(2):
            cols = pl.ds(j * 128, 128)
            pltpu.make_async_copy(gate.at[:, cc, :, cols], wv.at[j, cc, :, :, pl.ds(0, 128)], w_sem).start()
            pltpu.make_async_copy(up.at[:, cc, :, cols], wv.at[j, cc, :, :, pl.ds(128, 128)], w_sem).start()
    for j in range(16):
        pltpu.make_async_copy(down.at[:, pl.ds(j * 512, 512)], dv.at[j], d_sem).start()

    bar = pltpu.get_barrier_semaphore()

    def greet(dev):
        pl.semaphore_signal(bar, inc=1, device_id=dev, device_id_type=MESH)

    same = x == y
    greet((xp, t))
    greet((xm, t))
    greet(at(x, y, z, sib))
    for k in range(4):
        @pl.when(jnp.logical_not(jnp.logical_and(same, y == k)))
        def _():
            greet(at(y, k, z, c))

        @pl.when(jnp.logical_not(jnp.logical_and(same, x == k)))
        def _():
            greet(at(k, x, z, c))

    def greet_plane(i, carry):
        q = (p + i) % 16
        greet((x, q * 2 + c))
        return carry

    lax.fori_loop(1, 16, greet_plane, 0)
    pl.semaphore_wait(bar, jnp.where(same, 24, 26))

    def act_first(r):
        for k in range(4):
            src = act.at[pl.ds(r * RB + k * Q, Q), :]
            dst = af.at[r, x, k, :, pl.ds(col, 256)]
            here = jnp.logical_and(same, y == k)

            @pl.when(here)
            def _():
                pltpu.make_async_copy(src, dst, a1_r.at[r]).start()

            @pl.when(jnp.logical_not(here))
            def _():
                send(src, dst, a1_s.at[r, k], a1_r.at[r], at(y, k, z, c))

    def act_first_done(r):
        wait_for(af.at[r, :, 0, :, pl.ds(0, 256)], a1_r.at[r])

    def act_a(r):
        for i in range(1, 4):
            piece = af.at[r, pl.ds(0, 2), y, :, pl.ds(col, 256)]
            send(piece, piece, ag_s.at[r, 0], ag_r.at[r, 0], at(x, (y + i) % 4, z, c))
            piece = af.at[r, pl.ds(2, 2), y, :, pl.ds(col, 256)]
            send(piece, piece, ag_s.at[r, 1], ag_r.at[r, 1], at(x, y, (z + i) % 4, c))

    def act_b(r):
        wait_for(af.at[r, pl.ds(0, 2), pl.ds(0, 3), :, pl.ds(0, 256)], ag_r.at[r, 0])
        for i in range(1, 4):
            piece = af.at[r, pl.ds(0, 2), :, :, pl.ds(col, 256)]
            send(piece, piece, ag_s.at[r, 2], ag_r.at[r, 2], at(x, y, (z + i) % 4, c))
        wait_for(af.at[r, pl.ds(2, 2), 0, :, pl.ds(0, 768)], ag_r.at[r, 1])
        for i in range(1, 4):
            piece = af.at[r, pl.ds(2, 2), y, :, pl.ds(ccol, 1024)]
            send(piece, piece, ag_s.at[r, 3], ag_r.at[r, 3], at(x, (y + i) % 4, z, c))

    def act_sib(r):
        wait_for(af.at[r, pl.ds(0, 2), :, :, pl.ds(0, 768)], ag_r.at[r, 2])
        wait_for(af.at[r, pl.ds(2, 2), pl.ds(0, 3), :, pl.ds(0, 1024)], ag_r.at[r, 3])
        piece = af.at[r, :, :, :, pl.ds(ccol, 1024)]
        send(piece, piece, ag_s.at[r, 4], ag_r.at[r, 4], at(x, y, z, sib))

    def act_done(r):
        wait_for(af.at[r, :, :, :, pl.ds(0, 1024)], ag_r.at[r, 4])

    def act_sent(r):
        for k in range(4):
            @pl.when(jnp.logical_not(jnp.logical_and(same, y == k)))
            def _():
                wait_for(af.at[r, 0, 0, :, pl.ds(0, 256)], a1_s.at[r, k])
        wait_for(af.at[r, pl.ds(0, 2), pl.ds(0, 3), :, pl.ds(0, 256)], ag_s.at[r, 0])
        wait_for(af.at[r, pl.ds(2, 2), 0, :, pl.ds(0, 768)], ag_s.at[r, 1])
        wait_for(af.at[r, pl.ds(0, 2), :, :, pl.ds(0, 768)], ag_s.at[r, 2])
        wait_for(af.at[r, pl.ds(2, 2), pl.ds(0, 3), :, pl.ds(0, 1024)], ag_s.at[r, 3])
        wait_for(af.at[r, :, :, :, pl.ds(0, 1024)], ag_s.at[r, 4])

    def multiply(r):
        def step(j, carry):
            w = wv[j].reshape(2048, 256)
            a = af[r].reshape(4 * RB, 2048)
            pacc[...] = jnp.dot(a, w, preferred_element_type=F32).reshape(4, RB, 256)
            far = pacc[(x + 2) % 4].astype(BF)
            xo[r, j, 0] = far[:HB]
            xo[r, j, 1] = far[HB:]
            send(xo.at[r, j, 0], ro.at[r, 0, j], xo_s.at[r], xo_r.at[r, 0, j], (xp, t))
            send(xo.at[r, j, 1], ro.at[r, 1, j], xo_s.at[r], xo_r.at[r, 1, j], (xm, t))
            nxt = pacc[xp]
            nb[0, j] = nxt[:HB]
            xn[r, 0, j, 1] = nxt[HB:].astype(BF)
            send(xn.at[r, 0, j, 1], rn.at[r, 0, j, 1], xn_s.at[r], xn_r.at[r, 0], (xp, t))
            prv = pacc[xm]
            nb[1, j] = prv[HB:]
            xn[r, 1, j, 0] = prv[:HB].astype(BF)
            send(xn.at[r, 1, j, 0], rn.at[r, 1, j, 0], xn_s.at[r], xn_r.at[r, 1], (xm, t))
            own[r, j] = pacc[x]
            return carry

        lax.fori_loop(0, TILES, step, 0)

    def relay(r):
        def step(j, carry):
            wait_for(ro.at[r, 0, j], xo_r.at[r, 0, j])
            xn[r, 0, j, 0] = (nb[0, j] + ro[r, 0, j].astype(F32)).astype(BF)
            send(xn.at[r, 0, j, 0], rn.at[r, 0, j, 0], xn_s.at[r], xn_r.at[r, 0], (xp, t))
            wait_for(ro.at[r, 1, j], xo_r.at[r, 1, j])
            xn[r, 1, j, 1] = (nb[1, j] + ro[r, 1, j].astype(F32)).astype(BF)
            send(xn.at[r, 1, j, 1], rn.at[r, 1, j, 1], xn_s.at[r], xn_r.at[r, 1], (xm, t))
            return carry

        lax.fori_loop(0, TILES, step, 0)

    def reduce_sent(r):
        wait_for(xo.at[r], xo_s.at[r])
        wait_for(xn.at[r], xn_s.at[r])

    def hide(r):
        wait_for(rn.at[r, 0], xn_r.at[r, 0])
        wait_for(rn.at[r, 1], xn_r.at[r, 1])
        groups = []
        for j in range(TILES):
            s = own[r, j] + rn[r, 0, j].reshape(RB, 256).astype(F32) + rn[r, 1, j].reshape(RB, 256).astype(F32)
            g, u = s[:, :128], s[:, 128:]
            groups.append((g / (1.0 + jnp.exp(-g)) * u).reshape(16, 8, 128))
        hs[r] = pack(groups)
        hr[r, c, p] = hs[r, p]

        def step(i, carry):
            q = (p + i) % 16
            send(hs.at[r, q], hr.at[r, c, p], h_s.at[r, 0], h_r.at[r, 0], (x, q * 2 + c))
            return carry

        lax.fori_loop(1, 16, step, 0)

    def hide_sib(r):
        wait_for(hs.at[r, pl.ds(0, 15)], h_r.at[r, 0])
        send(hr.at[r, c], hr.at[r, c], h_s.at[r, 1], h_r.at[r, 1], at(x, y, z, sib))

    def mix(r):
        wait_for(hs.at[r], h_r.at[r, 1])
        both = jnp.concatenate([unpack(hr[r, 0]), unpack(hr[r, 1])], axis=0)
        mixed = jnp.dot(both, mhi[...], preferred_element_type=F32)
        mixed = mixed + jnp.dot(both, mlo[...], preferred_element_type=F32)
        sign = jnp.where(c == 0, 1.0, -1.0).astype(F32)
        s = mixed[:128] + sign * mixed[128:]
        parts = [s[8 * i : 8 * i + 8] for i in range(16)]
        half = 1
        while half < 16:
            for i in range(16):
                if i & half == 0:
                    a, b = parts[i], parts[i + half]
                    parts[i], parts[i + half] = a + b, a - b
            half *= 2
        for i in range(16):
            rs[r, i] = pack([parts[i][None, :, 128 * g : 128 * g + 128] for g in range(TILES)])[0]
        rr[r, p] = rs[r, p]

        def step(i, carry):
            q = (p + i) % 16
            send(rs.at[r, q], rr.at[r, p], h_s.at[r, 2], h_r.at[r, 2], (x, q * 2 + c))
            return carry

        lax.fori_loop(1, 16, step, 0)

    def mix_sent(r):
        wait_for(hs.at[r, pl.ds(0, 15)], h_s.at[r, 0])
        wait_for(hs.at[r], h_s.at[r, 1])
        wait_for(hs.at[r, pl.ds(0, 15)], h_s.at[r, 2])

    def project(r):
        wait_for(rr.at[r, pl.ds(0, 15)], h_r.at[r, 2])
        rot[...] = unpack(rr[r])

        def step(i, carry):
            d = jnp.dot(rot[...], dv[i], preferred_element_type=F32)
            left, right = d[:, :256], d[:, 256:]
            dk[i] = jnp.where(c == 0, left, right)
            ds[r, i] = jnp.where(c == 0, right, left).astype(BF)
            send(ds.at[r, i], dr.at[r, i], ds_s.at[r], ds_r.at[r, i], at(x, y, z, sib))
            return carry

        lax.fori_loop(0, 16, step, 0)

    def spread(r):
        def step(i, carry):
            wait_for(dr.at[r, i], ds_r.at[r, i])
            e = (dk[i] + dr[r, i].astype(F32)).astype(BF)
            es[r, 0, i // 4, i % 4] = e[:HB]
            es[r, 1, i // 4, i % 4] = e[HB:]
            return carry

        lax.fori_loop(0, 16, step, 0)
        for i in range(1, 4):
            zz, yy = (z + i) % 4, (y + i) % 4
            send(es.at[r, 0, :, zz], f1.at[r, 0, i - 1], e_s.at[r, 0], e_r.at[r, 0], at(x, y, zz, c))
            send(es.at[r, 1, yy], f1.at[r, 1, i - 1], e_s.at[r, 1], e_r.at[r, 1], at(x, yy, z, c))

    def gather_one(r):
        wait_for(f1.at[r, 0], e_r.at[r, 0])
        g0 = es[r, 0, :, z].astype(F32)
        for i in range(3):
            g0 = g0 + f1[r, 0, i].astype(F32)
        g2[r, 0] = g0.astype(BF)
        for i in range(1, 4):
            yy = (y + i) % 4
            send(g2.at[r, 0, yy], f2.at[r, 0, i - 1], e_s.at[r, 2], e_r.at[r, 2], at(x, yy, z, c))
        wait_for(f1.at[r, 1], e_r.at[r, 1])
        g1 = es[r, 1, y].astype(F32)
        for i in range(3):
            g1 = g1 + f1[r, 1, i].astype(F32)
        g2[r, 1] = g1.astype(BF)
        for i in range(1, 4):
            zz = (z + i) % 4
            send(g2.at[r, 1, zz], f2.at[r, 1, i - 1], e_s.at[r, 3], e_r.at[r, 3], at(x, y, zz, c))

    def finish(r):
        for h, own_block in ((0, y), (1, z)):
            wait_for(f2.at[r, h], e_r.at[r, 2 + h])
            total = g2[r, h, own_block].astype(F32)
            for i in range(3):
                total = total + f2[r, h, i].astype(F32)
            out[pl.ds(r * RB + h * HB, HB), :] = total.astype(BF)

    def project_sent(r):
        wait_for(ds.at[r], ds_s.at[r])
        wait_for(f1.at[r, 0], e_s.at[r, 0])
        wait_for(f1.at[r, 1], e_s.at[r, 1])
        wait_for(f2.at[r, 0], e_s.at[r, 2])
        wait_for(f2.at[r, 1], e_s.at[r, 3])

    act_first(0)
    act_first(1)

    def build(i, carry):
        f_in = i * 128 + lax.broadcasted_iota(jnp.int32, (128, SPAN), 0)
        f_out = lax.broadcasted_iota(jnp.int32, (128, SPAN), 1)
        b_in, b_out = (f_in * 9363) >> 16, (f_out * 9363) >> 16
        a_in, a_out = f_in - 7 * b_in, f_out - 7 * b_out
        v = b_in & b_out
        v = v ^ (v >> 4)
        v = v ^ (v >> 2)
        v = v ^ (v >> 1)
        sign = (1 - 2 * (v & 1)).astype(F32)
        value = jnp.zeros((128, SPAN), F32)
        a_row = a_out[:8]
        for k in range(7):
            row = jnp.zeros((8, SPAN), F32)
            for m in range(7):
                row = jnp.where(a_row == m, gm[m, k], row)
            value = jnp.where(a_in == k, row[:1], value)
        value = value * sign * (1.0 / 64.0)
        hi = value.astype(BF)
        rows = pl.ds(pl.multiple_of(i * 128, 128), 128)
        mhi[rows, :] = hi
        mlo[rows, :] = (value - hi.astype(F32)).astype(BF)
        return carry

    lax.fori_loop(0, TILES, build, 0)

    act_first_done(0)
    act_a(0)
    act_first_done(1)
    act_a(1)
    act_b(0)
    act_b(1)
    act_sib(0)
    wait_for(wv, w_sem)
    act_done(0)
    multiply(0)
    act_sib(1)
    relay(0)
    act_done(1)
    multiply(1)
    hide(0)
    relay(1)
    hide_sib(0)
    mix(0)
    wait_for(dv, d_sem)
    project(0)
    spread(0)
    gather_one(0)
    hide(1)
    hide_sib(1)
    finish(0)
    mix(1)
    project(1)
    spread(1)
    gather_one(1)
    finish(1)
    for r in range(CHUNKS):
        act_sent(r)
        reduce_sent(r)
        mix_sent(r)
        project_sent(r)


def local(activations, gate_weight, up_weight, group_mix, down_weight):
    any_space = pl.BlockSpec(memory_space=pl.ANY)
    dma = pltpu.SemaphoreType.DMA
    vm = pltpu.VMEM
    r = CHUNKS
    scratch = [
        vm((TILES, 2, 4, 256, 256), BF),
        vm((16, SPAN, 512), BF),
        vm((r, 4, 4, Q, 2048), BF),
        vm((4, RB, 256), F32),
        vm((r, TILES, RB, 256), F32),
        vm((2, TILES, HB, 256), F32),
        vm((r, TILES, 2, HB, 256), BF),
        vm((r, 2, TILES, 2, HB, 256), BF),
        vm((r, 2, TILES, HB, 256), BF),
        vm((r, 2, TILES, 2, HB, 256), BF),
        vm((SPAN, SPAN), BF),
        vm((SPAN, SPAN), BF),
        vm((r, 16, 64, 128), BF),
        vm((r, 2, 16, 64, 128), BF),
        vm((r, 16, 64, 128), BF),
        vm((r, 16, 64, 128), BF),
        vm((RB, SPAN), BF),
        vm((r, 16, RB, 256), BF),
        vm((16, RB, 256), F32),
        vm((r, 16, RB, 256), BF),
        vm((r, 2, 4, 4, HB, 256), BF),
        vm((r, 2, 3, 4, HB, 256), BF),
        vm((r, 2, 4, HB, 256), BF),
        vm((r, 2, 3, HB, 256), BF),
        dma(()), dma(()),
        dma((r, 4)), dma((r,)),
        dma((r, 5)), dma((r, 5)),
        dma((r,)), dma((r, 2, TILES)),
        dma((r,)), dma((r, 2)),
        dma((r, 3)), dma((r, 3)),
        dma((r,)), dma((r, 16)),
        dma((r, 4)), dma((r, 4)),
    ]
    return pl.pallas_call(
        kernel,
        out_shape=jax.ShapeDtypeStruct((256, 256), BF),
        in_specs=[any_space, any_space, any_space, pl.BlockSpec(memory_space=pltpu.SMEM), any_space],
        out_specs=pl.BlockSpec(memory_space=pltpu.VMEM),
        scratch_shapes=scratch,
        compiler_params=pltpu.CompilerParams(
            collective_id=0, has_side_effects=True, vmem_limit_bytes=60 * 1024 * 1024
        ),
        cost_estimate=pl.CostEstimate(flops=12_000_000_000, bytes_accessed=24_000_000, transcendentals=230_000),
        name="ffn",
    )(
        activations,
        gate_weight.reshape(4, 2, 256, SPAN),
        up_weight.reshape(4, 2, 256, SPAN),
        group_mix,
        down_weight,
    )


def solution(mesh):
    return jax.shard_map(
        local,
        mesh=mesh,
        in_specs=(P("dp", "tensor"), P("dp", "tensor"), P("dp", "tensor"), P(), P("tensor", None)),
        out_specs=P("dp", "tensor"),
        check_vma=False,
    )
```

time: 414 us -> 120 us (0.29)
  waiting for transfers between devices: 294 us -> 0 us
  Pallas kernels: 0 us -> 117 us
  blocking collectives: 54.3 us -> 0 us
  matrix products: 24.7 us -> 0 us
  between operations: 13.2 us -> 0.01 us
  starting transfers between devices: 9.32 us -> 0 us
  local copies, waits for them, and re-layouts: 9.28 us -> 1.57 us
  other arithmetic: 7.46 us -> 0 us
    reduce_scatter x2 -> x0, waiting for transfers between devices: 164 us -> none  [the longest x1 93.6 us: local(): lax.psum_scatter(down_terms, 'tensor', scatter_dimension=1, tiled=True)]
    pallas_call x0 -> x1, Pallas kernels: none -> 117 us  [local(): pl.pallas_call(kernel, out_shape=jax.ShapeDtypeStruct((256, 256), BF), in...]
    ppermute x5 -> x0, waiting for transfers between devices: 78.6 us -> none  [swapped(): lax.ppermute(array, axis, [(i, i ^ 1 << stride) for i in range(lax.axis_s...]
    all_to_all x1 -> x0, blocking collectives: 54.3 us -> none  [local(): lax.all_to_all(feature_rows, 'dp', split_axis=1, concat_axis=0, tiled=True)]
    all_gather x1 -> x0, waiting for transfers between devices: 51.4 us -> none  [local(): feature_rows = lax.all_gather(activations, 'tensor', axis=1, tiled=True)]
    dot_general x5 -> x0, matrix products: 24.7 us -> none  [the longest x1 12.1 us: local(): jnp.dot(rotated, down_weight, preferred_element_type=jnp.float32)]
    ppermute x5 -> x0, starting transfers between devices: 9.24 us -> none  [swapped(): lax.ppermute(array, axis, [(i, i ^ 1 << stride) for i in range(lax.axis_s...]
    all_to_all x1 -> x0, local copies, waits for them, and re-layouts: 6.34 us -> none  [local(): lax.all_to_all(feature_rows, 'dp', split_axis=1, concat_axis=0, tiled=True)]
  transfers between devices with their start and end apart: 8 -> 0, of which waited for: 8 -> 0; matrix products, arithmetic and copies ran while one was open for 0% -> 0% of each run, Pallas kernels for 0% -> 0%
where the time goes in v1:
time: 120 us; the launch traced here: 119 us
  Pallas kernels  117 us (98%)
  local copies, waits for them, and re-layouts  1.57 us (1%)
    pallas_call x1, Pallas kernels, local(): pl.pallas_call(kernel, out_shape=jax.ShapeDtypeStruct((256, 256), BF), in...  117 us

profile of v1, /device:TPU:1, one launch (start us, length us, event | category | flops | bytes accessed | tf_op | source)
XLA Modules:
  0.0 119.0 jit_solution(12532674421608096817)
XLA Ops:
  0.0 117.5 %ffn.1 = bf16[256,256]{1,0:T(8,128)(2,1)} custom-call(bf16[256,256]{1,0:T(8,128)(2,1)} %act.1, bf16[4,2,256,896]{3,2,1,0:T(8,128)(2,1)} %bitcast.2, bf16[4,2,256,896]{3,2,1,0:T(8,128)(2,1)} %bitcast.3, f32[7,7]{1,0:T(8,128)} %gm.1, bf16[896,8192]{1,0:T(8,128)(2,1)} %down.1), custom_call_target="tpu_custom_call" | custom-call | flops 12000000000 | bytes 24000000 | tf_op jit(solution)/shard_map/ffn/pallas_call | solution.py:414
  117.5 1.6 %copy.7 = bf16[256,256]{1,0:T(8,128)(2,1)} copy(bf16[256,256]{1,0:T(8,128)(2,1)} %ffn.1) | data formatting | bytes 262144

commit v2 on v1

--- a/solution.py
+++ b/solution.py
@@ -9,12 +9,17 @@
 BF = jnp.bfloat16
 F32 = jnp.float32
 
-CHUNKS = 2
+CHUNKS = 4
 RB = 256 // CHUNKS
+PARTS = 2
+PER = CHUNKS // PARTS
+RT = 256 // PARTS
+HT = RT // 2
 Q = RB // 4
 HB = RB // 2
 TILES = 7
 SPAN = 896
+LAG = 4
 GROUPS = 8
 
 
@@ -70,9 +75,6 @@
             cols = pl.ds(j * 128, 128)
             pltpu.make_async_copy(gate.at[:, cc, :, cols], wv.at[j, cc, :, :, pl.ds(0, 128)], w_sem).start()
             pltpu.make_async_copy(up.at[:, cc, :, cols], wv.at[j, cc, :, :, pl.ds(128, 128)], w_sem).start()
-    for j in range(16):
-        pltpu.make_async_copy(down.at[:, pl.ds(j * 512, 512)], dv.at[j], d_sem).start()
-
     bar = pltpu.get_barrier_semaphore()
 
     def greet(dev):
@@ -91,13 +93,14 @@
         def _():
             greet(at(k, x, z, c))
 
-    def greet_plane(i, carry):
-        q = (p + i) % 16
-        greet((x, q * 2 + c))
-        return carry
-
-    lax.fori_loop(1, 16, greet_plane, 0)
-    pl.semaphore_wait(bar, jnp.where(same, 24, 26))
+    for k in range(1, 4):
+        greet(at(x, (y + k) % 4, z, c))
+        greet(at(x, y, (z + k) % 4, c))
+    pl.semaphore_wait(bar, jnp.where(same, 15, 17))
+
+    def down_start():
+        for j in range(16):
+            pltpu.make_async_copy(down.at[:, pl.ds(j * 512, 512)], dv.at[j], d_sem).start()
 
     def act_first(r):
         for k in range(4):
@@ -164,11 +167,11 @@
             send(xo.at[r, j, 0], ro.at[r, 0, j], xo_s.at[r], xo_r.at[r, 0, j], (xp, t))
             send(xo.at[r, j, 1], ro.at[r, 1, j], xo_s.at[r], xo_r.at[r, 1, j], (xm, t))
             nxt = pacc[xp]
-            nb[0, j] = nxt[:HB]
+            nb[r, 0, j] = nxt[:HB]
             xn[r, 0, j, 1] = nxt[HB:].astype(BF)
             send(xn.at[r, 0, j, 1], rn.at[r, 0, j, 1], xn_s.at[r], xn_r.at[r, 0], (xp, t))
             prv = pacc[xm]
-            nb[1, j] = prv[HB:]
+            nb[r, 1, j] = prv[HB:]
             xn[r, 1, j, 0] = prv[:HB].astype(BF)
             send(xn.at[r, 1, j, 0], rn.at[r, 1, j, 0], xn_s.at[r], xn_r.at[r, 1], (xm, t))
             own[r, j] = pacc[x]
@@ -179,10 +182,10 @@
     def relay(r):
         def step(j, carry):
             wait_for(ro.at[r, 0, j], xo_r.at[r, 0, j])
-            xn[r, 0, j, 0] = (nb[0, j] + ro[r, 0, j].astype(F32)).astype(BF)
+            xn[r, 0, j, 0] = (nb[r, 0, j] + ro[r, 0, j].astype(F32)).astype(BF)
             send(xn.at[r, 0, j, 0], rn.at[r, 0, j, 0], xn_s.at[r], xn_r.at[r, 0], (xp, t))
             wait_for(ro.at[r, 1, j], xo_r.at[r, 1, j])
-            xn[r, 1, j, 1] = (nb[1, j] + ro[r, 1, j].astype(F32)).astype(BF)
+            xn[r, 1, j, 1] = (nb[r, 1, j] + ro[r, 1, j].astype(F32)).astype(BF)
             send(xn.at[r, 1, j, 1], rn.at[r, 1, j, 1], xn_s.at[r], xn_r.at[r, 1], (xm, t))
             return carry
 
@@ -193,22 +196,30 @@
         wait_for(xn.at[r], xn_s.at[r])
 
     def hide(r):
+        part, first = r // PER, (r % PER) * (16 // PER)
         wait_for(rn.at[r, 0], xn_r.at[r, 0])
         wait_for(rn.at[r, 1], xn_r.at[r, 1])
         groups = []
         for j in range(TILES):
             s = own[r, j] + rn[r, 0, j].reshape(RB, 256).astype(F32) + rn[r, 1, j].reshape(RB, 256).astype(F32)
             g, u = s[:, :128], s[:, 128:]
-            groups.append((g / (1.0 + jnp.exp(-g)) * u).reshape(16, 8, 128))
-        hs[r] = pack(groups)
-        hr[r, c, p] = hs[r, p]
+            groups.append((g / (1.0 + jnp.exp(-g)) * u).reshape(RB // 8, 8, 128))
+        hs[part, first : first + 16 // PER] = pack(groups)
 
         def step(i, carry):
-            q = (p + i) % 16
-            send(hs.at[r, q], hr.at[r, c, p], h_s.at[r, 0], h_r.at[r, 0], (x, q * 2 + c))
-            return carry
-
-        lax.fori_loop(1, 16, step, 0)
+            q = first + (p + i) % (16 // PER)
+
+            @pl.when(q != p)
+            def _():
+                send(hs.at[part, q], hr.at[part, c, p], h_s.at[part, 0], h_r.at[part, 0], (x, q * 2 + c))
+
+            @pl.when(q == p)
+            def _():
+                hr[part, c, p] = hs[part, p]
+
+            return carry
+
+        lax.fori_loop(0, 16 // PER, step, 0)
 
     def hide_sib(r):
         wait_for(hs.at[r, pl.ds(0, 15)], h_r.at[r, 0])
@@ -249,29 +260,45 @@
         wait_for(rr.at[r, pl.ds(0, 15)], h_r.at[r, 2])
         rot[...] = unpack(rr[r])
 
+        def spread(i):
+            q = (p + 1 + i) % 16
+            qy, qz = q // 4, q % 4
+            wait_for(dr.at[r, q], ds_r.at[r, q])
+            e = (dk[q] + dr[r, q].astype(F32)).astype(BF)
+            es[r, 0, qy, qz] = e[:HT]
+            es[r, 1, qy, qz] = e[HT:]
+
+            @pl.when(qz != z)
+            def _():
+                slot = (qz + 3 - z) % 4
+                send(es.at[r, 0, qy, qz], f1.at[r, 0, slot, qy], e_s.at[r, 0], e_r.at[r, 0], at(x, y, qz, c))
+
+            @pl.when(qy != y)
+            def _():
+                slot = (qy + 3 - y) % 4
+                send(es.at[r, 1, qy, qz], f1.at[r, 1, slot, qz], e_s.at[r, 1], e_r.at[r, 1], at(x, qy, z, c))
+
         def step(i, carry):
-            d = jnp.dot(rot[...], dv[i], preferred_element_type=F32)
+            q = (p + 1 + i) % 16
+            d = jnp.dot(rot[...], dv[q], preferred_element_type=F32)
             left, right = d[:, :256], d[:, 256:]
-            dk[i] = jnp.where(c == 0, left, right)
-            ds[r, i] = jnp.where(c == 0, right, left).astype(BF)
-            send(ds.at[r, i], dr.at[r, i], ds_s.at[r], ds_r.at[r, i], at(x, y, z, sib))
+            dk[q] = jnp.where(c == 0, left, right)
+            ds[r, q] = jnp.where(c == 0, right, left).astype(BF)
+            send(ds.at[r, q], dr.at[r, q], ds_s.at[r], ds_r.at[r, q], at(x, y, z, sib))
+
+            @pl.when(i >= LAG)
+            def _():
+                spread(i - LAG)
+
             return carry
 
         lax.fori_loop(0, 16, step, 0)
 
-    def spread(r):
-        def step(i, carry):
-            wait_for(dr.at[r, i], ds_r.at[r, i])
-            e = (dk[i] + dr[r, i].astype(F32)).astype(BF)
-            es[r, 0, i // 4, i % 4] = e[:HB]
-            es[r, 1, i // 4, i % 4] = e[HB:]
-            return carry
-
-        lax.fori_loop(0, 16, step, 0)
-        for i in range(1, 4):
-            zz, yy = (z + i) % 4, (y + i) % 4
-            send(es.at[r, 0, :, zz], f1.at[r, 0, i - 1], e_s.at[r, 0], e_r.at[r, 0], at(x, y, zz, c))
-            send(es.at[r, 1, yy], f1.at[r, 1, i - 1], e_s.at[r, 1], e_r.at[r, 1], at(x, yy, z, c))
+        def last(i, carry):
+            spread(i)
+            return carry
+
+        lax.fori_loop(16 - LAG, 16, last, 0)
 
     def gather_one(r):
         wait_for(f1.at[r, 0], e_r.at[r, 0])
@@ -297,7 +324,7 @@
             total = g2[r, h, own_block].astype(F32)
             for i in range(3):
                 total = total + f2[r, h, i].astype(F32)
-            out[pl.ds(r * RB + h * HB, HB), :] = total.astype(BF)
+            out[pl.ds(r * RT + h * HT, HT), :] = total.astype(BF)
 
     def project_sent(r):
         wait_for(ds.at[r], ds_s.at[r])
@@ -306,8 +333,8 @@
         wait_for(f2.at[r, 0], e_s.at[r, 2])
         wait_for(f2.at[r, 1], e_s.at[r, 3])
 
-    act_first(0)
-    act_first(1)
+    for r in range(CHUNKS):
+        act_first(r)
 
     def build(i, carry):
         f_in = i * 128 + lax.broadcasted_iota(jnp.int32, (128, SPAN), 0)
@@ -340,34 +367,50 @@
     act_first_done(1)
     act_a(1)
     act_b(0)
+    act_first_done(2)
+    act_a(2)
     act_b(1)
     act_sib(0)
+    act_first_done(3)
+    act_a(3)
+    act_b(2)
+    down_start()
     wait_for(wv, w_sem)
     act_done(0)
     multiply(0)
     act_sib(1)
-    relay(0)
+    act_b(3)
     act_done(1)
     multiply(1)
+    act_sib(2)
+    relay(0)
+    act_done(2)
+    multiply(2)
+    act_sib(3)
+    relay(1)
     hide(0)
-    relay(1)
+    act_done(3)
+    multiply(3)
+    relay(2)
+    hide(1)
+    relay(3)
     hide_sib(0)
     mix(0)
+    hide(2)
+    hide(3)
     wait_for(dv, d_sem)
     project(0)
-    spread(0)
+    hide_sib(1)
+    mix(1)
     gather_one(0)
-    hide(1)
-    hide_sib(1)
+    project(1)
     finish(0)
-    mix(1)
-    project(1)
-    spread(1)
     gather_one(1)
     finish(1)
     for r in range(CHUNKS):
         act_sent(r)
         reduce_sent(r)
+    for r in range(PARTS):
         mix_sent(r)
         project_sent(r)
 
@@ -376,40 +419,40 @@
     any_space = pl.BlockSpec(memory_space=pl.ANY)
     dma = pltpu.SemaphoreType.DMA
     vm = pltpu.VMEM
-    r = CHUNKS
+    r, n = CHUNKS, PARTS
     scratch = [
         vm((TILES, 2, 4, 256, 256), BF),
         vm((16, SPAN, 512), BF),
         vm((r, 4, 4, Q, 2048), BF),
         vm((4, RB, 256), F32),
         vm((r, TILES, RB, 256), F32),
-        vm((2, TILES, HB, 256), F32),
+        vm((r, 2, TILES, HB, 256), F32),
         vm((r, TILES, 2, HB, 256), BF),
         vm((r, 2, TILES, 2, HB, 256), BF),
         vm((r, 2, TILES, HB, 256), BF),
         vm((r, 2, TILES, 2, HB, 256), BF),
         vm((SPAN, SPAN), BF),
         vm((SPAN, SPAN), BF),
-        vm((r, 16, 64, 128), BF),
-        vm((r, 2, 16, 64, 128), BF),
-        vm((r, 16, 64, 128), BF),
-        vm((r, 16, 64, 128), BF),
-        vm((RB, SPAN), BF),
-        vm((r, 16, RB, 256), BF),
-        vm((16, RB, 256), F32),
-        vm((r, 16, RB, 256), BF),
-        vm((r, 2, 4, 4, HB, 256), BF),
-        vm((r, 2, 3, 4, HB, 256), BF),
-        vm((r, 2, 4, HB, 256), BF),
-        vm((r, 2, 3, HB, 256), BF),
+        vm((n, 16, 64, 128), BF),
+        vm((n, 2, 16, 64, 128), BF),
+        vm((n, 16, 64, 128), BF),
+        vm((n, 16, 64, 128), BF),
+        vm((RT, SPAN), BF),
+        vm((n, 16, RT, 256), BF),
+        vm((16, RT, 256), F32),
+        vm((n, 16, RT, 256), BF),
+        vm((n, 2, 4, 4, HT, 256), BF),
+        vm((n, 2, 3, 4, HT, 256), BF),
+        vm((n, 2, 4, HT, 256), BF),
+        vm((n, 2, 3, HT, 256), BF),
         dma(()), dma(()),
         dma((r, 4)), dma((r,)),
         dma((r, 5)), dma((r, 5)),
         dma((r,)), dma((r, 2, TILES)),
         dma((r,)), dma((r, 2)),
-        dma((r, 3)), dma((r, 3)),
-        dma((r,)), dma((r, 16)),
-        dma((r, 4)), dma((r, 4)),
+        dma((n, 3)), dma((n, 3)),
+        dma((n,)), dma((n, 16)),
+        dma((n, 4)), dma((n, 4)),
     ]
     return pl.pallas_call(
         kernel,

time: 120 us -> 98.8 us (0.82)
  Pallas kernels: 117 us -> 96.7 us
    pallas_call x1, Pallas kernels: 117 us -> 96.7 us  [local(): pl.pallas_call(kernel, out_shape=jax.ShapeDtypeStruct((256, 256), BF), in...]
where the time goes in v2:
time: 98.8 us; the launch traced here: 98.3 us
  Pallas kernels  96.7 us (98%)
  local copies, waits for them, and re-layouts  1.57 us (2%)
    pallas_call x1, Pallas kernels, local(): pl.pallas_call(kernel, out_shape=jax.ShapeDtypeStruct((256, 256), BF), in...  96.7 us

profile of v2, /device:TPU:1, one launch (start us, length us, event | category | flops | bytes accessed | tf_op | source)
XLA Modules:
  0.0 98.3 jit_solution(10575453554181041559)
XLA Ops:
  0.0 96.7 %ffn.1 = bf16[256,256]{1,0:T(8,128)(2,1)} custom-call(bf16[256,256]{1,0:T(8,128)(2,1)} %act.1, bf16[4,2,256,896]{3,2,1,0:T(8,128)(2,1)} %bitcast.2, bf16[4,2,256,896]{3,2,1,0:T(8,128)(2,1)} %bitcast.3, f32[7,7]{1,0:T(8,128)} %gm.1, bf16[896,8192]{1,0:T(8,128)(2,1)} %down.1), custom_call_target="tpu_custom_call" | custom-call | flops 12000000000 | bytes 24000000 | tf_op jit(solution)/shard_map/ffn/pallas_call | solution.py:457
  96.7 1.6 %copy.7 = bf16[256,256]{1,0:T(8,128)(2,1)} copy(bf16[256,256]{1,0:T(8,128)(2,1)} %ffn.1) | data formatting | bytes 262144

commit v3 on v2

v3 whole, which is shorter than its diff:
```python
import jax
import jax.numpy as jnp
from jax import lax
from jax.experimental import pallas as pl
from jax.experimental.pallas import tpu as pltpu
from jax.sharding import PartitionSpec as P

MESH = pl.DeviceIdType.MESH
BF = jnp.bfloat16
F32 = jnp.float32

CHUNKS = 4
RB = 256 // CHUNKS
PARTS = ((0, 1), (2,), (3,))
PART_OF = [k for k, part in enumerate(PARTS) for _ in part]
ROWS = [RB * len(part) for part in PARTS]
OFF = [RB * part[0] for part in PARTS]
LAST = len(PARTS) - 1
PIECE = [rows // 16 for rows in ROWS]
PK = [8 * piece for piece in PIECE]
Q = RB // 4
HB = RB // 2
TILES = 7
SPAN = 896
LAG = 4
GROUPS = 8


def wait_for(ref, sem):
    pltpu.make_async_copy(ref, ref, sem).wait()


def cross(a, b):
    low = lax.broadcasted_iota(jnp.int32, a.shape, a.ndim - 2) < 4
    half_turn = lambda v: jnp.concatenate([v[..., 4:, :], v[..., :4, :]], axis=-2)
    return jnp.where(low, a, half_turn(b)), jnp.where(low, half_turn(a), b)


def pack(groups, piece):
    rows = groups[0].shape[0]
    groups = [g.reshape(rows // 8, 8, 128) for g in groups]
    groups.append(jnp.zeros_like(groups[0]))
    if piece == 8:
        pairs = [jnp.concatenate(groups[i : i + 2], axis=1) for i in range(0, GROUPS, 2)]
        return jnp.concatenate([v.astype(BF) for v in pairs], axis=1)
    even, odd = zip(*[cross(groups[i], groups[i + 1]) for i in range(0, GROUPS, 2)])
    both = jnp.stack([jnp.concatenate(even, axis=1), jnp.concatenate(odd, axis=1)], axis=1)
    return both.reshape(rows // 4, 32, 128).astype(BF)


def unpack(packed, piece):
    out = []
    if piece == 8:
        for i in range(0, GROUPS, 2):
            pair = packed[:, i * 8 : i * 8 + 16, :].astype(F32)
            out += [pair[:, :8, :].reshape(128, 128), pair[:, 8:, :].reshape(128, 128)]
    else:
        both = packed.astype(F32).reshape(8, 2, 32, 128)
        for i in range(0, GROUPS, 2):
            rows = slice(4 * i, 4 * i + 8)
            first, second = cross(both[:, 0, rows], both[:, 1, rows])
            out += [first.reshape(64, 128), second.reshape(64, 128)]
    return jnp.concatenate([v.astype(BF) for v in out[:TILES]], axis=1)


def kernel(
    act, gate, up, gm, down, out,
    wv, dv, af, pacc, own, nb, xo, xn, ro, rn,
    mhi, mlo, hs, hr, rs, rr, rot, ds, dk, dr, es, f1, g2, f2, ed, fd,
    w_sem, d_sem, a1_s, a1_r, ag_s, ag_r, xo_s, xo_r, xn_s, xn_r,
    h_s, h_r, ds_s, ds_r, e_s, e_r, a0_r, ao_s, ao_r,
):
    x = lax.axis_index("dp")
    t = lax.axis_index("tensor")
    y, z, c = t // 8, (t // 2) % 4, t % 2
    p = t // 2
    sib = 1 - c
    xp, xm = (x + 1) % 4, (x + 3) % 4
    kb, kbs = c * 4 + z, pl.ds(c * 4, 4)

    def at(x_, y_, z_, c_):
        return (x_, y_ * 8 + z_ * 2 + c_)

    def send(src, dst, ss, rs_, dev):
        pltpu.make_async_remote_copy(
            src_ref=src, dst_ref=dst, send_sem=ss, recv_sem=rs_, device_id=dev, device_id_type=MESH
        ).start()

    for j in range(TILES):
        for cc in range(2):
            cols = pl.ds(j * 128, 128)
            pltpu.make_async_copy(gate.at[:, cc, :, cols], wv.at[j, cc, :, :, pl.ds(0, 128)], w_sem).start()
            pltpu.make_async_copy(up.at[:, cc, :, cols], wv.at[j, cc, :, :, pl.ds(128, 128)], w_sem).start()
    bar = pltpu.get_barrier_semaphore()

    def greet(dev):
        pl.semaphore_signal(bar, inc=1, device_id=dev, device_id_type=MESH)

    same = x == y
    greet((xp, t))
    greet((xm, t))
    greet(at(x, y, z, sib))
    for k in range(4):
        @pl.when(jnp.logical_not(jnp.logical_and(same, y == k)))
        def _():
            greet(at(y, k, z, c))

        @pl.when(jnp.logical_not(jnp.logical_and(same, x == k)))
        def _():
            greet(at(k, x, z, c))


    def greet_plane(i, carry):
        greet((x, (p + i) % 16 * 2 + c))
        return carry

    lax.fori_loop(1, 16, greet_plane, 0)
    pl.semaphore_wait(bar, jnp.where(same, 24, 26))

    def down_start():
        for j in range(16):
            pltpu.make_async_copy(down.at[:, pl.ds(j * 512, 512)], dv.at[j], d_sem).start()

    def act_first(r):
        sem = a0_r.at[x] if r == 0 else a1_r.at[r]
        for k in range(4):
            src = act.at[pl.ds(r * RB + k * Q, Q), :]
            dst = af.at[r, x, kb, k]
            here = jnp.logical_and(same, y == k)

            @pl.when(here)
            def _():
                pltpu.make_async_copy(src, dst, sem).start()

            @pl.when(jnp.logical_not(here))
            def _():
                send(src, dst, a1_s.at[r, k], sem, at(y, k, z, c))

    def act_first_done(r):
        wait_for(af.at[r, :, 0, 0], a1_r.at[r])

    def act_a(r):
        for i in range(1, 4):
            piece = af.at[r, pl.ds(0, 2), kb, y]
            send(piece, piece, ag_s.at[r, 0], ag_r.at[r, 0], at(x, (y + i) % 4, z, c))
            piece = af.at[r, pl.ds(2, 2), kb, y]
            send(piece, piece, ag_s.at[r, 1], ag_r.at[r, 1], at(x, y, (z + i) % 4, c))

    def act_b(r):
        wait_for(af.at[r, pl.ds(0, 2), 0, pl.ds(0, 3)], ag_r.at[r, 0])
        for i in range(1, 4):
            piece = af.at[r, pl.ds(0, 2), kb]
            send(piece, piece, ag_s.at[r, 2], ag_r.at[r, 2], at(x, y, (z + i) % 4, c))
        wait_for(af.at[r, pl.ds(0, 2), 0, pl.ds(0, 3)], ag_r.at[r, 1])
        for i in range(1, 4):
            piece = af.at[r, pl.ds(2, 2), kbs, y]
            send(piece, piece, ag_s.at[r, 3], ag_r.at[r, 3], at(x, (y + i) % 4, z, c))

    def act_sib(r):
        wait_for(af.at[r, pl.ds(0, 2), pl.ds(0, 3)], ag_r.at[r, 2])
        wait_for(af.at[r, pl.ds(0, 2), pl.ds(0, 3)], ag_r.at[r, 3])
        piece = af.at[r, :, kbs]
        send(piece, piece, ag_s.at[r, 4], ag_r.at[r, 4], at(x, y, z, sib))

    def block(i):
        a, b = i // 4, i % 4
        dy, dz = (3 * a * a + 3 * a + 6) % 7 % 4, (3 * b * b + 3 * b + 6) % 7 % 4
        return ((y + dy) % 4) * 4 + (z + dz) % 4

    def own0_first(o):
        wait_for(af.at[0, 0, 0, 0], a0_r.at[(x + o) % 4])

    def own0_a(o):
        piece = af.at[0, (x + o) % 4, kb, y]

        def step(i, carry):
            send(piece, piece, ao_s.at[o, 0], ao_r.at[o, 0], (x, block(i) * 2 + c))
            return carry

        lax.fori_loop(0, 15, step, 0)

    def own0_sib(o):
        wait_for(af.at[0, pl.ds(0, 3), pl.ds(0, 5), 0], ao_r.at[o, 0])
        piece = af.at[0, (x + o) % 4, kbs]
        send(piece, piece, ao_s.at[o, 1], ao_r.at[o, 1], at(x, y, z, sib))

    def own0_done(o):
        wait_for(af.at[0, 0, pl.ds(0, 4)], ao_r.at[o, 1])

    def act_done(r):
        wait_for(af.at[r, :, pl.ds(0, 4)], ag_r.at[r, 4])

    def act_sent(r):
        for k in range(4):
            @pl.when(jnp.logical_not(jnp.logical_and(same, y == k)))
            def _():
                wait_for(af.at[r, 0, 0, 0], a1_s.at[r, k])
        if r == 0:
            for o in range(4):
                wait_for(af.at[0, pl.ds(0, 3), pl.ds(0, 5), 0], ao_s.at[o, 0])
                wait_for(af.at[0, 0, pl.ds(0, 4)], ao_s.at[o, 1])
            return
        wait_for(af.at[r, pl.ds(0, 2), 0, pl.ds(0, 3)], ag_s.at[r, 0])
        wait_for(af.at[r, pl.ds(0, 2), 0, pl.ds(0, 3)], ag_s.at[r, 1])
        wait_for(af.at[r, pl.ds(0, 2), pl.ds(0, 3)], ag_s.at[r, 2])
        wait_for(af.at[r, pl.ds(0, 2), pl.ds(0, 3)], ag_s.at[r, 3])
        wait_for(af.at[r, :, pl.ds(0, 4)], ag_s.at[r, 4])

    def direct_tile(r, j):
        send(xn.at[r, 0, j, 1], rn.at[r, 0, j, 1], xn_s.at[r], xn_r.at[r, 0], (xp, t))
        send(xn.at[r, 1, j, 0], rn.at[r, 1, j, 0], xn_s.at[r], xn_r.at[r, 1], (xm, t))

    def far_tile(r, j, far):
        xo[r, j, 0] = far[:HB]
        xo[r, j, 1] = far[HB:]
        send(xo.at[r, j, 0], ro.at[r, 0, j], xo_s.at[r], xo_r.at[r, 0, j], (xp, t))
        send(xo.at[r, j, 1], ro.at[r, 1, j], xo_s.at[r], xo_r.at[r, 1, j], (xm, t))

    def multiply_far(r, start, stop):
        def step(j, carry):
            a = jnp.concatenate([af[r, (x + 2) % 4, b].reshape(RB, 256) for b in range(8)], axis=1)
            far_tile(r, j, jnp.dot(a, wv[j].reshape(2048, 256), preferred_element_type=F32).astype(BF))
            return carry

        lax.fori_loop(start, stop, step, 0)

    def multiply(r, at_once):
        def step(j, carry):
            w = wv[j].reshape(2048, 256)
            a = jnp.concatenate([af[r, :, b].reshape(4 * RB, 256) for b in range(8)], axis=1)
            pacc[...] = jnp.dot(a, w, preferred_element_type=F32).reshape(4, RB, 256)
            if r > 0:
                far_tile(r, j, pacc[(x + 2) % 4].astype(BF))
            nxt = pacc[xp]
            nb[r, 0, j] = nxt[:HB]
            xn[r, 0, j, 1] = nxt[HB:].astype(BF)
            prv = pacc[xm]
            nb[r, 1, j] = prv[HB:]
            xn[r, 1, j, 0] = prv[:HB].astype(BF)
            if at_once:
                direct_tile(r, j)
            own[r, j] = pacc[x]
            return carry

        lax.fori_loop(0, TILES, step, 0)

    def direct(r):
        def step(j, carry):
            direct_tile(r, j)
            return carry

        lax.fori_loop(0, TILES, step, 0)

    def relay(r):
        def step(j, carry):
            wait_for(ro.at[r, 0, j], xo_r.at[r, 0, j])
            xn[r, 0, j, 0] = (nb[r, 0, j] + ro[r, 0, j].astype(F32)).astype(BF)
            send(xn.at[r, 0, j, 0], rn.at[r, 0, j, 0], xn_s.at[r], xn_r.at[r, 0], (xp, t))
            wait_for(ro.at[r, 1, j], xo_r.at[r, 1, j])
            xn[r, 1, j, 1] = (nb[r, 1, j] + ro[r, 1, j].astype(F32)).astype(BF)
            send(xn.at[r, 1, j, 1], rn.at[r, 1, j, 1], xn_s.at[r], xn_r.at[r, 1], (xm, t))
            return carry

        lax.fori_loop(0, TILES, step, 0)

    def reduce_sent(r):
        wait_for(xo.at[r], xo_s.at[r])
        wait_for(xn.at[r], xn_s.at[r])

    def pieces(ref, k, count):
        return ref.at[k, pl.ds(0, count * PK[k])]

    def piece_of(k, q):
        return pl.ds(pl.multiple_of(q * PK[k], PK[k]), PK[k])

    def hide(r):
        k = PART_OF[r]
        count = RB // PIECE[k]
        first = (r - PARTS[k][0]) * count
        wait_for(rn.at[r, 0], xn_r.at[r, 0])
        wait_for(rn.at[r, 1], xn_r.at[r, 1])
        groups = []
        for j in range(TILES):
            s = own[r, j] + rn[r, 0, j].reshape(RB, 256).astype(F32) + rn[r, 1, j].reshape(RB, 256).astype(F32)
            g, u = s[:, :128], s[:, 128:]
            groups.append(g / (1.0 + jnp.exp(-g)) * u)
        hs[k, pl.ds(first * PK[k], count * PK[k])] = pack(groups, PIECE[k]).reshape(count * PK[k], 128)
        mine = piece_of(k, p)

        def step(i, carry):
            q = first + (p + i) % count

            @pl.when(q != p)
            def _():
                send(hs.at[k, piece_of(k, q)], hr.at[k, c, mine], h_s.at[k, 0], h_r.at[k, 0], (x, q * 2 + c))

            @pl.when(q == p)
            def _():
                hr[k, c, mine] = hs[k, mine]

            return carry

        lax.fori_loop(0, count, step, 0)

    def hide_sib(k):
        wait_for(pieces(hs, k, 15), h_r.at[k, 0])
        both = hr.at[k, c, pl.ds(0, 16 * PK[k])]
        send(both, both, h_s.at[k, 1], h_r.at[k, 1], at(x, y, z, sib))

    def mix(k):
        n, piece, every, mine = ROWS[k], PIECE[k], pl.ds(0, 16 * PK[k]), piece_of(k, p)
        wait_for(pieces(hs, k, 16), h_r.at[k, 1])
        both = jnp.concatenate([unpack(hr[k, i, every].reshape(16, PK[k], 128), piece) for i in range(2)], axis=0)
        mixed = jnp.dot(both, mhi[...], preferred_element_type=F32)
        mixed = mixed + jnp.dot(both, mlo[...], preferred_element_type=F32)
        sign = jnp.where(c == 0, 1.0, -1.0).astype(F32)
        s = mixed[:n] + sign * mixed[n:]
        if piece == 4:
            v = s.reshape(8, 8, SPAN)
            turned = jnp.concatenate([v[:, 4:], v[:, :4]], axis=1)
            low = lax.broadcasted_iota(jnp.int32, v.shape, 1) < 4
            s = jnp.where(low, v + turned, turned - v).reshape(n, SPAN)
        parts = [s[8 * i : 8 * i + 8] for i in range(n // 8)]
        half = 1
        while half < len(parts):
            for i in range(len(parts)):
                if i & half == 0:
                    a, b = parts[i], parts[i + half]
                    parts[i], parts[i + half] = a + b, a - b
            half *= 2
        for i in range(len(parts)):
            groups = [parts[i][:, 128 * g : 128 * g + 128] for g in range(TILES)]
            rs[k, pl.ds(i * 64, 64)] = pack(groups, piece).reshape(64, 128)
        rr[k, mine] = rs[k, mine]

        def step(i, carry):
            q = (p + i) % 16
            send(rs.at[k, piece_of(k, q)], rr.at[k, mine], h_s.at[k, 2], h_r.at[k, 2], (x, q * 2 + c))
            return carry

        lax.fori_loop(1, 16, step, 0)

    def mix_sent(k):
        wait_for(pieces(hs, k, 15), h_s.at[k, 0])
        wait_for(pieces(hs, k, 16), h_s.at[k, 1])
        wait_for(pieces(hs, k, 15), h_s.at[k, 2])

    def spread(k, i):
        h, rows, halves, top = ROWS[k] // 2, pl.ds(OFF[k], ROWS[k]), pl.ds(OFF[k] // 2, ROWS[k] // 2), pl.ds(0, ROWS[k])
        q = block(i)
        qy, qz = q // 4, q % 4
        wait_for(dr.at[q, rows], ds_r.at[k, q])
        e = (dk[q, top] + dr[q, rows].astype(F32)).astype(BF)
        if k == LAST:
            ed[q] = e

            @pl.when(i < 15)
            def _():
                send(ed.at[q], fd.at[p], e_s.at[k, 0], e_r.at[k, 0], (x, q * 2 + c))

            return
        es[0, qy, qz, halves] = e[:h]
        es[1, qy, qz, halves] = e[h:]

        @pl.when(qz != z)
        def _():
            slot = (qz + 3 - z) % 4
            dst = f1.at[0, slot, qy, halves]
            send(es.at[0, qy, qz, halves], dst, e_s.at[k, 0], e_r.at[k, 0], at(x, y, qz, c))

        @pl.when(qy != y)
        def _():
            slot = (qy + 3 - y) % 4
            dst = f1.at[1, slot, qz, halves]
            send(es.at[1, qy, qz, halves], dst, e_s.at[k, 1], e_r.at[k, 1], at(x, qy, z, c))

    def project(k, start, stop):
        rows, top = pl.ds(OFF[k], ROWS[k]), pl.ds(0, ROWS[k])
        if start == 0:
            wait_for(pieces(rr, k, 15), h_r.at[k, 2])
            rot[top, :] = unpack(rr[k, pl.ds(0, 16 * PK[k])].reshape(16, PK[k], 128), PIECE[k])

        def step(i, carry):
            q = block(i)
            d = jnp.dot(rot[top, :], dv[q], preferred_element_type=F32)
            left, right = d[:, :256], d[:, 256:]
            dk[q, top] = jnp.where(c == 0, left, right)
            ds[q, rows] = jnp.where(c == 0, right, left).astype(BF)
            send(ds.at[q, rows], dr.at[q, rows], ds_s.at[k], ds_r.at[k, q], at(x, y, z, sib))

            @pl.when(i >= LAG)
            def _():
                spread(k, i - LAG)

            return carry

        lax.fori_loop(start, stop, step, 0)

    def flush(k):
        def step(i, carry):
            spread(k, i)
            return carry

        lax.fori_loop(16 - LAG, 16, step, 0)

    def gather_one(k):
        halves = pl.ds(OFF[k] // 2, ROWS[k] // 2)
        for a in range(2):
            wait_for(f1.at[a, :, :, halves], e_r.at[k, a])
            total = es[0, :, z, halves].astype(F32) if a == 0 else es[1, y, :, halves].astype(F32)
            for i in range(3):
                total = total + f1[a, i, :, halves].astype(F32)
            g2[a, :, halves] = total.astype(BF)
            for i in range(1, 4):
                q = (y + i) % 4 if a == 0 else (z + i) % 4
                dev = at(x, q, z, c) if a == 0 else at(x, y, q, c)
                send(g2.at[a, q, halves], f2.at[a, i - 1, halves], e_s.at[k, 2 + a], e_r.at[k, 2 + a], dev)

    def finish(k):
        h = ROWS[k] // 2
        if k == LAST:
            wait_for(ed.at[pl.ds(0, 15)], e_r.at[k, 0])
            fd[p] = ed[p]
            total = fd[0].astype(F32)
            for i in range(1, 16):
                total = total + fd[i].astype(F32)
            out[pl.ds(OFF[k], ROWS[k]), :] = total.astype(BF)
            return
        halves = pl.ds(OFF[k] // 2, h)
        for a, own_block in ((0, y), (1, z)):
            wait_for(f2.at[a, :, halves], e_r.at[k, 2 + a])
            total = g2[a, own_block, halves].astype(F32)
            for i in range(3):
                total = total + f2[a, i, halves].astype(F32)
            out[pl.ds(OFF[k] + a * h, h), :] = total.astype(BF)

    def project_sent(k):
        halves = pl.ds(OFF[k] // 2, ROWS[k] // 2)
        wait_for(ds.at[:, pl.ds(OFF[k], ROWS[k])], ds_s.at[k])
        if k == LAST:
            wait_for(ed.at[pl.ds(0, 15)], e_s.at[k, 0])
            return
        for a in range(2):
            wait_for(f1.at[a, :, :, halves], e_s.at[k, a])
            wait_for(f2.at[a, :, halves], e_s.at[k, 2 + a])

    for r in range(CHUNKS):
        act_first(r)

    def build(i, carry):
        f_in = i * 128 + lax.broadcasted_iota(jnp.int32, (128, SPAN), 0)
        f_out = lax.broadcasted_iota(jnp.int32, (128, SPAN), 1)
        b_in, b_out = (f_in * 9363) >> 16, (f_out * 9363) >> 16
        a_in, a_out = f_in - 7 * b_in, f_out - 7 * b_out
        v = b_in & b_out
        v = v ^ (v >> 4)
        v = v ^ (v >> 2)
        v = v ^ (v >> 1)
        sign = (1 - 2 * (v & 1)).astype(F32)
        value = jnp.zeros((128, SPAN), F32)
        a_row = a_out[:8]
        for k in range(7):
            row = jnp.zeros((8, SPAN), F32)
            for m in range(7):
                row = jnp.where(a_row == m, gm[m, k], row)
            value = jnp.where(a_in == k, row[:1], value)
        value = value * sign * (1.0 / 64.0)
        hi = value.astype(BF)
        rows = pl.ds(pl.multiple_of(i * 128, 128), 128)
        mhi[rows, :] = hi
        mlo[rows, :] = (value - hi.astype(F32)).astype(BF)
        return carry

    lax.fori_loop(0, TILES, build, 0)

    own0_first(2)
    own0_a(2)
    own0_first(1)
    own0_a(1)
    own0_first(3)
    own0_a(3)
    own0_first(0)
    own0_a(0)
    act_first_done(1)
    act_a(1)
    act_first_done(2)
    act_a(2)
    act_first_done(3)
    act_a(3)
    wait_for(wv, w_sem)
    own0_sib(2)
    own0_sib(1)
    own0_sib(3)
    act_b(1)
    own0_done(2)
    multiply_far(0, 0, 3)
    own0_sib(0)
    act_b(2)
    multiply_far(0, 3, 7)
    act_b(3)
    own0_done(1)
    own0_done(3)
    own0_done(0)
    multiply(0, True)
    act_sib(1)
    relay(0)
    act_sib(2)
    act_done(1)
    multiply(1, True)
    act_sib(3)
    act_done(2)
    multiply(2, False)
    relay(1)
    direct(2)
    hide(0)
    act_done(3)
    multiply(3, False)
    down_start()
    relay(2)
    direct(3)
    hide(1)
    relay(3)
    hide_sib(0)
    mix(0)
    hide(2)
    hide(3)
    hide_sib(1)
    mix(1)
    wait_for(dv, d_sem)
    project(0, 0, 8)
    hide_sib(2)
    project(0, 8, 12)
    mix(2)
    project(0, 12, 16)
    project(1, 0, 4)
    flush(0)
    project(1, 4, 16)
    gather_one(0)
    project(2, 0, 4)
    flush(1)
    project(2, 4, 16)
    flush(2)
    finish(0)
    gather_one(1)
    finish(1)
    finish(2)
    for r in range(CHUNKS):
        act_sent(r)
        reduce_sent(r)
    for r in range(len(PARTS)):
        mix_sent(r)
        project_sent(r)


def local(activations, gate_weight, up_weight, group_mix, down_weight):
    any_space = pl.BlockSpec(memory_space=pl.ANY)
    dma = pltpu.SemaphoreType.DMA
    vm = pltpu.VMEM
    r, n = CHUNKS, len(PARTS)
    scratch = [
        vm((TILES, 2, 4, 256, 256), BF),
        vm((16, SPAN, 512), BF),
        vm((r, 4, 8, 4, Q, 256), BF),
        vm((4, RB, 256), F32),
        vm((r, TILES, RB, 256), F32),
        vm((r, 2, TILES, HB, 256), F32),
        vm((r, TILES, 2, HB, 256), BF),
        vm((r, 2, TILES, 2, HB, 256), BF),
        vm((r, 2, TILES, HB, 256), BF),
        vm((r, 2, TILES, 2, HB, 256), BF),
        vm((SPAN, SPAN), BF),
        vm((SPAN, SPAN), BF),
        vm((n, 16 * 64, 128), BF),
        vm((n, 2, 16 * 64, 128), BF),
        vm((n, 16 * 64, 128), BF),
        vm((n, 16 * 64, 128), BF),
        vm((128, SPAN), BF),
        vm((16, 256, 256), BF),
        vm((16, 128, 256), F32),
        vm((16, 256, 256), BF),
        vm((2, 4, 4, 128, 256), BF),
        vm((2, 3, 4, 128, 256), BF),
        vm((2, 4, 128, 256), BF),
        vm((2, 3, 128, 256), BF),
        vm((16, ROWS[-1], 256), BF),
        vm((16, ROWS[-1], 256), BF),
        dma(()), dma(()),
        dma((r, 4)), dma((r,)),
        dma((r, 5)), dma((r, 5)),
        dma((r,)), dma((r, 2, TILES)),
        dma((r,)), dma((r, 2)),
        dma((n, 3)), dma((n, 3)),
        dma((n,)), dma((n, 16)),
        dma((n, 4)), dma((n, 4)),
        dma((4,)), dma((4, 2)), dma((4, 2)),
    ]
    return pl.pallas_call(
        kernel,
        out_shape=jax.ShapeDtypeStruct((256, 256), BF),
        in_specs=[any_space, any_space, any_space, pl.BlockSpec(memory_space=pltpu.SMEM), any_space],
        out_specs=pl.BlockSpec(memory_space=pltpu.VMEM),
        scratch_shapes=scratch,
        compiler_params=pltpu.CompilerParams(
            collective_id=0, has_side_effects=True, vmem_limit_bytes=60 * 1024 * 1024
        ),
        cost_estimate=pl.CostEstimate(flops=12_000_000_000, bytes_accessed=24_000_000, transcendentals=230_000),
        name="ffn",
    )(
        activations,
        gate_weight.reshape(4, 2, 256, SPAN),
        up_weight.reshape(4, 2, 256, SPAN),
        group_mix,
        down_weight,
    )


def solution(mesh):
    return jax.shard_map(
        local,
        mesh=mesh,
        in_specs=(P("dp", "tensor"), P("dp", "tensor"), P("dp", "tensor"), P(), P("tensor", None)),
        out_specs=P("dp", "tensor"),
        check_vma=False,
    )
```

time: 98.8 us -> 93.8 us (0.949)
  Pallas kernels: 96.7 us -> 92.1 us
    pallas_call x1, Pallas kernels: 96.7 us -> 92.1 us  [local(): pl.pallas_call(kernel, out_shape=jax.ShapeDtypeStruct((256, 256), BF), in...]
where the time goes in v3:
time: 93.8 us; the launch traced here: 93.7 us
  Pallas kernels  92.1 us (98%)
  local copies, waits for them, and re-layouts  1.57 us (2%)
    pallas_call x1, Pallas kernels, local(): pl.pallas_call(kernel, out_shape=jax.ShapeDtypeStruct((256, 256), BF), in...  92.1 us

profile of v3, /device:TPU:1, one launch (start us, length us, event | category | flops | bytes accessed | tf_op | source)
XLA Modules:
  0.0 93.7 jit_solution(16935207322743176191)
XLA Ops:
  0.0 92.1 %ffn.1 = bf16[256,256]{1,0:T(8,128)(2,1)} custom-call(bf16[256,256]{1,0:T(8,128)(2,1)} %act.1, bf16[4,2,256,896]{3,2,1,0:T(8,128)(2,1)} %bitcast.2, bf16[4,2,256,896]{3,2,1,0:T(8,128)(2,1)} %bitcast.3, f32[7,7]{1,0:T(8,128)} %gm.1, bf16[896,8192]{1,0:T(8,128)(2,1)} %down.1), custom_call_target="tpu_custom_call" | custom-call | flops 12000000000 | bytes 24000000 | tf_op jit(solution)/shard_map/ffn/pallas_call | solution.py:597
  92.1 1.6 %copy.7 = bf16[256,256]{1,0:T(8,128)(2,1)} copy(bf16[256,256]{1,0:T(8,128)(2,1)} %ffn.1) | data formatting | bytes 262144

commit v4 on v3

--- a/solution.py
+++ b/solution.py
@@ -22,7 +22,7 @@
 HB = RB // 2
 TILES = 7
 SPAN = 896
-LAG = 4
+LAG = 3
 GROUPS = 8
 
 

time: 93.8 us -> 93.5 us (level)
  no operation moved by 1% of the time
where the time goes in v4:
time: 93.5 us; the launch traced here: 93.3 us
  Pallas kernels  91.7 us (98%)
  local copies, waits for them, and re-layouts  1.57 us (2%)
    pallas_call x1, Pallas kernels, local(): pl.pallas_call(kernel, out_shape=jax.ShapeDtypeStruct((256, 256), BF), in...  91.7 us

profile of v4, /device:TPU:1, one launch (start us, length us, event | category | flops | bytes accessed | tf_op | source)
XLA Modules:
  0.0 93.3 jit_solution(7119842631749056329)
XLA Ops:
  0.0 91.7 %ffn.1 = bf16[256,256]{1,0:T(8,128)(2,1)} custom-call(bf16[256,256]{1,0:T(8,128)(2,1)} %act.1, bf16[4,2,256,896]{3,2,1,0:T(8,128)(2,1)} %bitcast.2, bf16[4,2,256,896]{3,2,1,0:T(8,128)(2,1)} %bitcast.3, f32[7,7]{1,0:T(8,128)} %gm.1, bf16[896,8192]{1,0:T(8,128)(2,1)} %down.1), custom_call_target="tpu_custom_call" | custom-call | flops 12000000000 | bytes 24000000 | tf_op jit(solution)/shard_map/ffn/pallas_call | solution.py:597
  91.7 1.6 %copy.7 = bf16[256,256]{1,0:T(8,128)(2,1)} copy(bf16[256,256]{1,0:T(8,128)(2,1)} %ffn.1) | data formatting | bytes 262144

commit v5 on v3

--- a/solution.py
+++ b/solution.py
@@ -532,9 +532,8 @@
     project(0, 8, 12)
     mix(2)
     project(0, 12, 16)
-    project(1, 0, 4)
     flush(0)
-    project(1, 4, 16)
+    project(1, 0, 16)
     gather_one(0)
     project(2, 0, 4)
     flush(1)

time: 93.8 us -> 94.5 us (level)
  no operation moved by 1% of the time
where the time goes in v5:
time: 94.5 us; the launch traced here: 94.4 us
  Pallas kernels  92.8 us (98%)
  local copies, waits for them, and re-layouts  1.57 us (2%)
    pallas_call x1, Pallas kernels, local(): pl.pallas_call(kernel, out_shape=jax.ShapeDtypeStruct((256, 256), BF), in...  92.8 us

profile of v5, /device:TPU:1, one launch (start us, length us, event | category | flops | bytes accessed | tf_op | source)
XLA Modules:
  0.0 94.4 jit_solution(5068897243452018201)
XLA Ops:
  0.0 92.8 %ffn.1 = bf16[256,256]{1,0:T(8,128)(2,1)} custom-call(bf16[256,256]{1,0:T(8,128)(2,1)} %act.1, bf16[4,2,256,896]{3,2,1,0:T(8,128)(2,1)} %bitcast.2, bf16[4,2,256,896]{3,2,1,0:T(8,128)(2,1)} %bitcast.3, f32[7,7]{1,0:T(8,128)} %gm.1, bf16[896,8192]{1,0:T(8,128)(2,1)} %down.1), custom_call_target="tpu_custom_call" | custom-call | flops 12000000000 | bytes 24000000 | tf_op jit(solution)/shard_map/ffn/pallas_call | solution.py:596
  92.8 1.6 %copy.7 = bf16[256,256]{1,0:T(8,128)(2,1)} copy(bf16[256,256]{1,0:T(8,128)(2,1)} %ffn.1) | data formatting | bytes 262144
